TPU v7x, 32 devices: a whole 2x2x4 slice. The times are simulated.
32 devices in a mesh: member: 2 (over y), patch: 4 (over x, core), chan: 4 (over z).
Axes of the slice: x: 2, y: 2, z: 4, core: 2. Of those that a mesh axis runs over, the one named last changes fastest.
Arguments:
- grid_latent: bfloat16 [1024, 8192], P('member', 'patch'), parts along dimension 0, may hold values from -6 to 6
- mesh_latent: bfloat16 [1024, 6144], P('member', 'patch'), parts along dimension 0, may hold values from -6 to 6
- edge_sender: int32 [4, 4, 1024], P('patch'), may hold values from 0 to 2047
- edge_receiver: int32 [4, 4, 1024], P(None, 'patch'), may hold values from 0 to 1535
- edge_count: int32 [4, 4], replicated, may hold values from 0 to 1024, as said below
- nbr_index: int32 [16, 6144], P(None, 'patch'), may hold values from 0 to 1791, as said below
- halo_send: int32 [4, 2, 128], P('patch'), may hold values from 0 to 1535
- w_edge_send: bfloat16 [512, 512], P(None, 'chan'), may hold values from -0.25 to 0.25
- w_edge_recv: bfloat16 [512, 512], P(None, 'chan'), may hold values from -0.25 to 0.25
- b_edge: float32 [512], P('chan'), may hold values from -4 to 4
- w_edge_out: bfloat16 [512, 512], P('chan'), may hold values from -0.125 to 0.125
- ln_gain: float32 [512], replicated, may hold values from 0.5 to 1.5
- w_query: bfloat16 [512, 512], replicated, may hold values from -1 to 1
- w_key: bfloat16 [512, 512], replicated, may hold values from -1 to 1
- w_value: bfloat16 [512, 512], P(None, 'chan'), may hold values from -0.25 to 0.25
- w_attn_out: bfloat16 [512, 512], P('chan'), may hold values from -0.25 to 0.25
Outputs:
- mesh_out: bfloat16 [1024, 6144], P('member', 'patch'), parts along dimension 0
There are 2 independent parts, one for each index of `member`. A program takes and returns all parts, laid end to end along the dimension named above; an argument that names none is the same for every part. Nothing has to cross between parts.
Inputs may be any that keep to these rules, and one draw needn't show every extreme that they name: edge_sender[b, p, c] is a row among band b's 2048 grid points; only slots c < edge_count[b, p] hold edges. edge_receiver[b, p, c] is a node among patch p's 1536 mesh nodes. edge_count[b, p] edges go from band b to patch p; in every draw some patch receives 1024 from every band. `nbr_index`: read as in the neighbour step. halo_send[p, 0] are the nodes of patch p offered to the patch before it, halo_send[p, 1] those offered to the patch after it.
All inputs are finite; a program needn't handle non-finite values.
Results may differ from a plain program's by a relative error of at most 0.0072.
Values may be sent and summed in bfloat16 or wider, within the bound.
A program may use at most 128 MiB of HBM per device.

v0:
```python
import jax
import jax.numpy as jnp
from jax import lax
from jax.sharding import PartitionSpec as P

HEADS = 4


def with_halo(cells, sides, width):
    for axis, dim in sides:
        count = lax.axis_size(axis)
        head = lax.slice_in_dim(cells, 0, width, axis=dim)
        tail = lax.slice_in_dim(cells, cells.shape[dim] - width, cells.shape[dim], axis=dim)
        cells = jnp.concatenate(
            [
                lax.ppermute(tail, axis, [(i, (i + 1) % count) for i in range(count)]),
                cells,
                lax.ppermute(head, axis, [((i + 1) % count, i) for i in range(count)]),
            ],
            axis=dim,
        )
    return cells


def contract(weight, operand):
    return lax.dot_general(
        weight, operand, (((0,), (0,)), ((), ())), preferred_element_type=jnp.float32
    )


def layer_norm(encoded, ln_gain):
    average = jnp.mean(encoded, axis=0, keepdims=True)
    centred = encoded - average
    variance = jnp.mean(centred * centred, axis=0, keepdims=True)
    return (centred * lax.rsqrt(variance + 1e-05) * ln_gain[:, None]).astype(jnp.bfloat16)


def per_device(
    grid_latent,
    mesh_latent,
    edge_sender,
    edge_receiver,
    edge_count,
    nbr_index,
    halo_send,
    w_edge_send,
    w_edge_recv,
    b_edge,
    w_edge_out,
    ln_gain,
    w_query,
    w_key,
    w_value,
    w_attn_out,
):
    patch_pos = lax.axis_index("patch")
    chan_pos = lax.axis_index("chan")
    model_width = mesh_latent.shape[0]
    mesh_rows = mesh_latent.shape[1]
    capacity = edge_sender.shape[2]
    halo_rows = halo_send.shape[2]
    neighbours = nbr_index.shape[0]
    width_dev = w_value.shape[1]
    hidden_units = w_edge_send.shape[1]
    send_rows = edge_sender[0]
    target_rows = edge_receiver[:, 0, :]
    counts_in = jnp.take(edge_count, patch_pos, axis=1)
    usable = jnp.arange(capacity, dtype=jnp.int32)[None, :] < counts_in[:, None]
    receiver_terms = contract(w_edge_recv, mesh_latent).astype(jnp.bfloat16)
    sender_terms = contract(w_edge_send, grid_latent).astype(jnp.bfloat16)
    outgoing = jnp.take(sender_terms, send_rows, axis=1)
    edge_terms = lax.all_to_all(outgoing, "patch", split_axis=1, concat_axis=1, tiled=True)
    summed = (
        edge_terms.astype(jnp.float32)
        + jnp.take(receiver_terms, target_rows, axis=1).astype(jnp.float32)
        + b_edge[:, None, None]
    )
    hidden = jnp.where(usable[None], jax.nn.silu(summed), 0.0).astype(jnp.bfloat16)
    node_acc = (
        jnp.zeros((hidden_units, mesh_rows), jnp.float32)
        .at[:, target_rows.reshape(-1)]
        .add(hidden.reshape(hidden_units, -1).astype(jnp.float32))
    )
    node_sum = node_acc.astype(jnp.bfloat16)
    encoded = mesh_latent.astype(jnp.float32) + lax.psum(contract(w_edge_out, node_sum), "chan")
    normed = layer_norm(encoded, ln_gain)
    query_nodes = contract(normed, w_query).astype(jnp.bfloat16)
    key_nodes = contract(normed, w_key).astype(jnp.bfloat16)
    value_nodes = contract(normed, w_value).astype(jnp.bfloat16)
    key_value = jnp.concatenate([key_nodes, value_nodes], axis=1)
    offered = jnp.take(key_value, halo_send[0].reshape(-1), axis=0)
    extended = with_halo(offered, (("patch", 0),), halo_rows)
    key_table = jnp.concatenate(
        [key_value, extended[:halo_rows], extended[3 * halo_rows :]], axis=0
    )
    head_size = model_width // HEADS
    my_dims = chan_pos * width_dev + jnp.arange(width_dev, dtype=jnp.int32)
    head_pick = (
        my_dims[:, None] // head_size == jnp.arange(HEADS, dtype=jnp.int32)[None, :]
    ).astype(jnp.bfloat16)
    block_rows = 512

    def attend(first_row):
        query_block = lax.dynamic_slice_in_dim(query_nodes, first_row, block_rows, 0).reshape(
            block_rows, HEADS, head_size
        )
        chosen = lax.dynamic_slice_in_dim(nbr_index, first_row, block_rows, 1).reshape(-1)
        picked = jnp.take(key_table, chosen, axis=0)
        key_block = picked[:, :model_width].reshape(neighbours, block_rows, HEADS, head_size)
        value_block = picked[:, model_width:].reshape(neighbours, block_rows, width_dev)
        scores = jnp.einsum(
            "bhd,kbhd->hkb", query_block, key_block, preferred_element_type=jnp.float32
        ) * head_size ** (-0.5)
        weights = jax.nn.softmax(scores, axis=1).astype(jnp.bfloat16)
        spread = jnp.einsum(
            "dh,hkb->kbd", head_pick, weights, preferred_element_type=jnp.float32
        ).astype(jnp.bfloat16)
        return jnp.einsum(
            "kbd,kbd->bd", spread, value_block, preferred_element_type=jnp.float32
        ).astype(jnp.bfloat16)

    starts = jnp.arange(mesh_rows // block_rows, dtype=jnp.int32) * block_rows
    blended_nodes = lax.map(attend, starts).reshape(mesh_rows, width_dev)
    blended_rows = blended_nodes.T
    mesh_out = encoded + lax.psum(contract(w_attn_out, blended_rows), "chan")
    return mesh_out.astype(jnp.bfloat16)


def solution(mesh):
    in_specs = (
        P("member", "patch"),
        P("member", "patch"),
        P("patch", None, None),
        P(None, "patch", None),
        P(),
        P(None, "patch"),
        P("patch", None, None),
        P(None, "chan"),
        P(None, "chan"),
        P("chan"),
        P("chan", None),
        P(),
        P(),
        P(),
        P(None, "chan"),
        P("chan", None),
    )
    out_specs = P("member", "patch")
    return jax.shard_map(
        per_device, mesh=mesh, in_specs=in_specs, out_specs=out_specs, check_vma=False
    )
```

profile of v0, /device:TPU:0, one launch (start us, length us, event | category | flops | bytes accessed | tf_op | source)
XLA Modules:
  0.0 637.4 jit_solution(11569496006662664594)
XLA Ops:
  8.2 1.4 convolution_convert_fusion.4
  9.8 12.1 %gather_fusion.1 = bf16[4096,128]{1,0:T(8,128)(2,1)S(1)} fusion(bf16[128,2048]{0,1:T(8,128)(2,1)S(1)} %copy.25, s32[4096]{0:T(1024)S(1)} %broadcast_clamp_fusion.2), kind=kCustom, calls=%fused_computation.1 | custom fusion | bytes 2113536 | tf_op jit(solution)/shard_map/jit(_take)/gather | solution.py:71
  22.0 2.1 select_bitcast_fusion
  24.1 4.4 all-to-all-start
  29.6 12.1 %gather_fusion.2 = bf16[4096,128]{1,0:T(8,128)(2,1)S(1)} fusion(bf16[128,1536]{0,1:T(8,128)(2,1)S(1)} %copy.26, s32[4096]{0:T(1024)S(1)} %broadcast_clamp_fusion.1), kind=kCustom, calls=%fused_computation.2 | custom fusion | bytes 2113536 | tf_op jit(solution)/shard_map/jit(_take)/gather | solution.py:75
  41.7 1.9 all-to-all-done
  43.7 5.2 select_convert_fusion
  48.8 22.9 %scatter_custom_fusion = f32[128,1536]{0,1:T(8,128)S(1)} fusion(s32[4096]{0:T(1024)S(1)} %bitcast.119, bf16[128,4096]{0,1:T(8,128)(2,1)} %bitcast.111, f32[]{:T(128)} %constant.109.clone.1), kind=kCustom, calls=%fused_computation.47 | custom fusion | flops 1048576 | bytes 1835012 | tf_op jit(solution)/shard_map/scatter-add | solution.py:82
  71.8 2.2 convolution_bitcast_fusion.1
  74.9 121.6 %all-reduce.3.cloned.1.call-done = f32[512,1536]{0,1:T(8,128)} async-done(((f32[512,1536]{0,1:T(8,128)}), f32[512,1536]{0,1:T(8,128)}) %all-reduce.3.cloned.1.call-update) | async-done | bytes 3145744 | tf_op jit(solution)/shard_map/psum | solution.py:85
  196.5 2.4 fusion.21
  203.5 1.4 pad_maximum_fusion.1
  204.9 2.8 copy.27
  207.7 1.9 gather_fusion.3
  209.6 1.1 copy.28
  211.8 3.7 convolution_convert_fusion
  216.3 1.2 collective-permute-done
  217.4 1.6 pad_maximum_fusion
  219.0 3.3 copy.29
  222.3 276.5 %while.12 = (s32[]{:T(128)}, bf16[3,512,128]{2,1,0:T(8,128)(2,1)}, s32[3]{0:T(128)S(1)}, s32[16,1536]{1,0:T(8,128)}, bf16[1792,640]{1,0:T(8,128)(2,1)S(1)}, /*in...) while((s32[]{:T(128)}, bf16[3,512,128]{2,1,0:T(8,128)(2,1)}, ...), condition=%wide.region_7.8_spmd.clone, body=%wide.region_4.7_spmd.clone.sunk | while | flops 27444244 | bytes 94569128 | solution.py:123
  226.0 34.2 %gather_fusion = bf16[8192,640]{1,0:T(8,128)(2,1)} fusion(bf16[1792,640]{1,0:T(8,128)(2,1)S(1)} %get-tuple-element.182, s32[8192]{0:T(1024)S(1)} %broadcast_clamp_fusion.4), kind=kCustom, calls=%fused_computation.clone.clone.1 | custom fusion | bytes 21004288 | tf_op jit(solution)/shard_map/while/body/eval_jaxpr/jit(_take)/gather | solution.py:108
  260.2 11.7 %broadcast_select_fusion.3 = bf16[8192,640]{1,0:T(8,128)(2,1)} fusion(bf16[8192,640]{1,0:T(8,128)(2,1)} %gather_fusion, pred[8192]{0:T(1024)(128)(4,1)S(1)} %compare_and_fusion.5), kind=kLoop, calls=%fused_computation.7.clone.1 | loop fusion | flops 5242880 | bytes 20979712 | tf_op jit(solution)/shard_map/while/body/eval_jaxpr/jit(_take)/select_n | solution.py:108
  271.9 3.1 slice.41
  275.0 7.2 %slice.42 = bf16[8192,512]{1,0:T(8,128)(2,1)} slice(bf16[8192,640]{1,0:T(8,128)(2,1)} %broadcast_select_fusion.3), slice={[0:8192], [0:512]} | slice | bytes 16777216 | tf_op jit(solution)/shard_map/while/body/eval_jaxpr/slice | solution.py:109
  282.2 12.5 %reshape.363 = bf16[16,512,4,128]{3,2,1,0:T(4,128)(2,1)} reshape(bf16[8192,512]{1,0:T(8,128)(2,1)} %slice.42) | data formatting | bytes 16777216 | tf_op jit(solution)/shard_map/while/body/eval_jaxpr/reshape | solution.py:109
  294.8 1.2 constant_dynamic-slice_fusion.2
  296.9 13.2 %fusion.48 = f32[4,512,1,16]{3,2,1,0:T(1,128)S(1)} fusion(bf16[16,512,4,128]{3,2,1,0:T(4,128)(2,1)} %reshape.363, bf16[512,4,128,1]{2,1,0,3:T(4,128)(2,1)} %reshape.364), kind=kOutput, calls=%fused_computation.8.clone.1 | convolution fusion | flops 8388608 | bytes 9043968 | tf_op jit(solution)/shard_map/while/body/eval_jaxpr/bhd,kbhd->hkb/dot_general | solution.py:111
  311.3 2.7 fusion.50
  318.1 34.2 %gather_fusion = bf16[8192,640]{1,0:T(8,128)(2,1)} fusion(bf16[1792,640]{1,0:T(8,128)(2,1)S(1)} %get-tuple-element.182, s32[8192]{0:T(1024)S(1)} %broadcast_clamp_fusion.4), kind=kCustom, calls=%fused_computation.clone.clone.1 | custom fusion | bytes 21004288 | tf_op jit(solution)/shard_map/while/body/eval_jaxpr/jit(_take)/gather | solution.py:108
  352.3 11.7 %broadcast_select_fusion.3 = bf16[8192,640]{1,0:T(8,128)(2,1)} fusion(bf16[8192,640]{1,0:T(8,128)(2,1)} %gather_fusion, pred[8192]{0:T(1024)(128)(4,1)S(1)} %compare_and_fusion.5), kind=kLoop, calls=%fused_computation.7.clone.1 | loop fusion | flops 5242880 | bytes 20979712 | tf_op jit(solution)/shard_map/while/body/eval_jaxpr/jit(_take)/select_n | solution.py:108
  364.0 3.1 slice.41
  367.1 7.2 %slice.42 = bf16[8192,512]{1,0:T(8,128)(2,1)} slice(bf16[8192,640]{1,0:T(8,128)(2,1)} %broadcast_select_fusion.3), slice={[0:8192], [0:512]} | slice | bytes 16777216 | tf_op jit(solution)/shard_map/while/body/eval_jaxpr/slice | solution.py:109
  374.4 12.5 %reshape.363 = bf16[16,512,4,128]{3,2,1,0:T(4,128)(2,1)} reshape(bf16[8192,512]{1,0:T(8,128)(2,1)} %slice.42) | data formatting | bytes 16777216 | tf_op jit(solution)/shard_map/while/body/eval_jaxpr/reshape | solution.py:109
  386.9 1.2 constant_dynamic-slice_fusion.2
  389.0 13.2 %fusion.48 = f32[4,512,1,16]{3,2,1,0:T(1,128)S(1)} fusion(bf16[16,512,4,128]{3,2,1,0:T(4,128)(2,1)} %reshape.363, bf16[512,4,128,1]{2,1,0,3:T(4,128)(2,1)} %reshape.364), kind=kOutput, calls=%fused_computation.8.clone.1 | convolution fusion | flops 8388608 | bytes 9043968 | tf_op jit(solution)/shard_map/while/body/eval_jaxpr/bhd,kbhd->hkb/dot_general | solution.py:111
  403.4 2.7 fusion.50
  410.2 34.2 %gather_fusion = bf16[8192,640]{1,0:T(8,128)(2,1)} fusion(bf16[1792,640]{1,0:T(8,128)(2,1)S(1)} %get-tuple-element.182, s32[8192]{0:T(1024)S(1)} %broadcast_clamp_fusion.4), kind=kCustom, calls=%fused_computation.clone.clone.1 | custom fusion | bytes 21004288 | tf_op jit(solution)/shard_map/while/body/eval_jaxpr/jit(_take)/gather | solution.py:108
  444.4 11.7 %broadcast_select_fusion.3 = bf16[8192,640]{1,0:T(8,128)(2,1)} fusion(bf16[8192,640]{1,0:T(8,128)(2,1)} %gather_fusion, pred[8192]{0:T(1024)(128)(4,1)S(1)} %compare_and_fusion.5), kind=kLoop, calls=%fused_computation.7.clone.1 | loop fusion | flops 5242880 | bytes 20979712 | tf_op jit(solution)/shard_map/while/body/eval_jaxpr/jit(_take)/select_n | solution.py:108
  456.1 3.1 slice.41
  459.2 7.2 %slice.42 = bf16[8192,512]{1,0:T(8,128)(2,1)} slice(bf16[8192,640]{1,0:T(8,128)(2,1)} %broadcast_select_fusion.3), slice={[0:8192], [0:512]} | slice | bytes 16777216 | tf_op jit(solution)/shard_map/while/body/eval_jaxpr/slice | solution.py:109
  466.5 12.5 %reshape.363 = bf16[16,512,4,128]{3,2,1,0:T(4,128)(2,1)} reshape(bf16[8192,512]{1,0:T(8,128)(2,1)} %slice.42) | data formatting | bytes 16777216 | tf_op jit(solution)/shard_map/while/body/eval_jaxpr/reshape | solution.py:109
  479.0 1.2 constant_dynamic-slice_fusion.2
  481.1 13.2 %fusion.48 = f32[4,512,1,16]{3,2,1,0:T(1,128)S(1)} fusion(bf16[16,512,4,128]{3,2,1,0:T(4,128)(2,1)} %reshape.363, bf16[512,4,128,1]{2,1,0,3:T(4,128)(2,1)} %reshape.364), kind=kOutput, calls=%fused_computation.8.clone.1 | convolution fusion | flops 8388608 | bytes 9043968 | tf_op jit(solution)/shard_map/while/body/eval_jaxpr/bhd,kbhd->hkb/dot_general | solution.py:111
  495.5 2.7 fusion.50
  498.8 3.3 convolution_bitcast_fusion
  502.1 120.3 %all-reduce.5.cloned.1.call-done = f32[512,1536]{0,1:T(8,128)} async-done(((f32[512,1536]{0,1:T(8,128)}), f32[512,1536]{0,1:T(8,128)}) %all-reduce.5.cloned.1.call-update) | async-done | bytes 3145744 | tf_op jit(solution)/shard_map/psum | solution.py:125
  622.4 5.5 add_convert_fusion
  628.0 2.6 copy.30
  (103 shorter events, 22.7 us)
Async XLA Ops:
  6.5 1.6 copy-start
  22.0 6.6 %copy-start.4 = (bf16[512,1536]{1,0:T(8,128)(2,1)S(1)}, bf16[512,1536]{1,0:T(8,128)(2,1)}, u32[]{:S(2)}) copy-start(bf16[512,1536]{1,0:T(8,128)(2,1)} %param.19) | copy-start | bytes 4718596
  22.0 6.6 %copy-start.9 = (bf16[512,128]{1,0:T(8,128)(2,1)S(1)}, bf16[512,128]{1,0:T(8,128)(2,1)}, u32[]{:S(2)}) copy-start(bf16[512,128]{1,0:T(8,128)(2,1)} %param.26) | copy-start | bytes 393220
  24.1 5.1 copy-start.8
  24.1 5.1 copy-start.13
  24.1 19.5 %all-to-all-start = ((bf16[128,4,1024]{0,2,1:T(8,128)(2,1)}), bf16[128,4,1024]{0,2,1:T(8,128)(2,1)}, u32[]{:S(2)}, u32[]{:S(2)}) async-start(bf16[128,4,1024]{0,2,1:T(8,128)(2,1)} %select_bitcast_fusion), calls=%async_computation | async-start | bytes 2097152 | tf_op jit(solution)/shard_map/all_to_all | solution.py:72
  28.5 168.0 %all-reduce.3.cloned.1.call-start = ((), (), s32[]{:S(2)}) async-start(), calls=%async_computation.1 | async-start | bytes 6291456 | tf_op jit(solution)/shard_map/psum | solution.py:85
  29.6 14.1 %copy-start.15 = (f32[128]{0:T(128)S(1)}, f32[128]{0:T(128)}, u32[]{:S(2)}) copy-start(f32[128]{0:T(128)} %param.27) | copy-start | bytes 1540
  43.7 28.1 %copy-start.10 = (bf16[128,512]{1,0:T(8,128)(2,1)S(1)}, bf16[128,512]{1,0:T(8,128)(2,1)}, u32[]{:S(2)}) copy-start(bf16[128,512]{1,0:T(8,128)(2,1)} %param.28) | copy-start | bytes 393220
  74.0 0.8 copy-start.14
  74.1 548.4 %all-reduce.5.cloned.1.call-start = ((), (), s32[]{:S(2)}) async-start(), calls=%async_computation.2 | async-start | bytes 6291456 | tf_op jit(solution)/shard_map/psum | solution.py:125
  74.8 125.3 %copy-start.3 = (bf16[512,1536]{0,1:T(8,128)(2,1)}, bf16[512,1536]{0,1:T(8,128)(2,1)S(1)}, u32[]{:S(2)}) copy-start(bf16[512,1536]{0,1:T(8,128)(2,1)S(1)} %copy.24) | copy-start | bytes 4718596
  196.5 2.8 copy-start.2
  199.3 0.8 copy-start.12
  200.2 1.1 copy-start.11
  200.2 2.2 copy-start.16
  201.3 1.1 copy-start.5
  202.4 1.0 copy-start.6
  210.9 5.4 collective-permute-start.1
  211.8 5.7 copy-start.7
  211.8 5.7 collective-permute-start
  622.4 8.1 %copy-start.1 = (bf16[512,2048]{1,0:T(8,128)(2,1)S(1)}, bf16[512,2048]{1,0:T(8,128)(2,1)}, u32[]{:S(2)}) copy-start(bf16[512,2048]{1,0:T(8,128)(2,1)} %param.18) | copy-start | bytes 6291460
Sparse Core Ops, SparseCore 0:
  74.2 122.3 all-reduce.2
  502.2 120.1 all-reduce.4
where the time goes:
time: 640 us; the launch traced here: 637 us
  waiting for transfers between devices  246 us (38%)
  local copies, waits for them, and re-layouts  224 us (35%)
  other arithmetic  82.3 us (13%)
  matrix products  60.4 us (9%)
  between operations  13.8 us (2%)
    psum x1, waiting for transfers between devices, per_device(): lax.psum(contract(w_edge_out, node_sum), 'chan')  122 us
    psum x1, waiting for transfers between devices, per_device(): mesh_out = encoded + lax.psum(contract(w_attn_out, blended_rows), 'chan')  120 us
    gather x3, local copies, waits for them, and re-layouts, attend(): picked = jnp.take(key_table, chosen, axis=0)  103 us
    dot_general x3, matrix products, attend(): jnp.einsum('bhd,kbhd->hkb', query_block, key_block, preferred_element_typ...  39.7 us
    reshape x3, local copies, waits for them, and re-layouts, attend(): picked[:, :model_width].reshape(neighbours, block_rows, HEADS, head_size)  37.6 us
    select_n x6, other arithmetic, attend(): picked = jnp.take(key_table, chosen, axis=0)  35.2 us
    scatter-add x1, other arithmetic, per_device(): node_acc = jnp.zeros((hidden_units, mesh_rows), jnp.float32).at[:, target...  22.9 us
    slice x3, local copies, waits for them, and re-layouts, attend(): picked[:, :model_width].reshape(neighbours, block_rows, HEADS, head_size)  21.7 us
  transfers between devices with their start and end apart: 5, of which 5 were waited for; matrix products, arithmetic and copies ran while one was open for 3% of the time, Pallas kernels for 0%

commit v1 on v0

v1 whole, which is shorter than its diff:
```python
import functools

import jax
import jax.numpy as jnp
from jax import lax
from jax.experimental import pallas as pl
from jax.experimental.pallas import tpu as pltpu
from jax.sharding import PartitionSpec as P

HEADS = 4
BF16 = jnp.bfloat16
F32 = jnp.float32
VMEM = pltpu.VMEM
QUERY_BLOCK = 256
NODE_BLOCK = 512
ONEHOT_ROWS = 256


def contract0(weight, operand):
    return lax.dot_general(
        weight, operand, (((0,), (0,)), ((), ())), preferred_element_type=F32
    )


def one_hot(first, rows, index_row):
    shape = (rows, index_row.shape[1])
    ids = lax.broadcasted_iota(jnp.int32, shape, 0)
    return jnp.where(ids == index_row - first, 1.0, 0.0).astype(BF16)


def call(body, out_shape, flops, nbytes, **kw):
    return pl.pallas_call(
        body,
        out_shape=out_shape,
        compiler_params=pltpu.CompilerParams(vmem_limit_bytes=40 * 2**20),
        cost_estimate=pl.CostEstimate(
            flops=int(flops), bytes_accessed=int(nbytes), transcendentals=0
        ),
        **kw,
    )


def pick_columns(table_ref, index_row):
    picked = None
    for first in range(0, table_ref.shape[1], ONEHOT_ROWS):
        term = jnp.dot(
            table_ref[:, first : first + ONEHOT_ROWS],
            one_hot(first, ONEHOT_ROWS, index_row),
            preferred_element_type=F32,
        )
        picked = term if picked is None else picked + term
    return picked


def project_and_pick(latent_ref, weight_ref, index_ref, out_ref, table_ref):
    @pl.when(pl.program_id(0) == 0)
    def _():
        table_ref[...] = contract0(weight_ref[...], latent_ref[...]).astype(BF16)

    index_row = index_ref[pl.ds(pl.program_id(0), 1), :]
    out_ref[0] = pick_columns(table_ref, index_row).astype(BF16)


def project_pick(latent, weight, index):
    blocks, cap = index.shape
    depth, width = weight.shape
    nodes = latent.shape[1]
    whole = lambda shape: pl.BlockSpec(shape, lambda j: (0,) * len(shape))
    return call(
        project_and_pick,
        jax.ShapeDtypeStruct((blocks, width, cap), BF16),
        2 * width * nodes * (depth + blocks * cap),
        2 * (latent.size + weight.size + blocks * width * cap),
        grid=(blocks,),
        in_specs=[whole(latent.shape), whole(weight.shape), whole(index.shape)],
        out_specs=pl.BlockSpec((1, width, cap), lambda j: (j, 0, 0)),
        scratch_shapes=[VMEM((width, nodes), BF16)],
    )(latent, weight, index)


def edge_sum_kernel(sent_ref, received_ref, bias_ref, index_ref, out_ref, acc_ref):
    step = pl.program_id(0)
    summed = sent_ref[0].astype(F32) + received_ref[0].astype(F32) + bias_ref[...]
    hidden = (summed / (1.0 + jnp.exp(-summed))).astype(BF16)
    index_row = index_ref[pl.ds(step, 1), :]
    nodes = acc_ref.shape[1]

    @pl.when(step == 0)
    def _():
        acc_ref[...] = jnp.zeros_like(acc_ref)

    for first in range(0, nodes, ONEHOT_ROWS):
        acc_ref[:, first : first + ONEHOT_ROWS] += lax.dot_general(
            hidden,
            one_hot(first, ONEHOT_ROWS, index_row),
            (((1,), (1,)), ((), ())),
            preferred_element_type=F32,
        )

    @pl.when(step == pl.num_programs(0) - 1)
    def _():
        out_ref[...] = acc_ref[...].astype(BF16)


def edge_sum(sent, received, bias, index, nodes):
    blocks, width, cap = sent.shape
    whole = lambda shape: pl.BlockSpec(shape, lambda j: (0,) * len(shape))
    block = pl.BlockSpec((1, width, cap), lambda j: (j, 0, 0))
    return call(
        edge_sum_kernel,
        jax.ShapeDtypeStruct((width, nodes), BF16),
        2 * width * nodes * blocks * cap,
        4 * sent.size,
        grid=(blocks,),
        in_specs=[block, block, whole(bias.shape), whole(index.shape)],
        out_specs=whole((width, nodes)),
        scratch_shapes=[VMEM((width, nodes), F32)],
    )(sent, received, bias, index)


def count_kernel(index_ref, out_ref):
    index = index_ref[...]
    slots, width = index.shape
    rows = 64
    ids = lax.broadcasted_iota(jnp.int32, (rows, width), 0)

    def body(step, carry):
        first = step * rows
        here = ids + first
        total = jnp.zeros((rows, width), F32)
        for slot in range(slots):
            total += jnp.where(here == index[slot : slot + 1, :], 1.0, 0.0)
        out_ref[pl.ds(pl.multiple_of(first, rows), rows), :] = total.astype(BF16)
        return carry

    lax.fori_loop(0, out_ref.shape[0] // rows, body, 0)


def count_slots(nbr_index, table_rows):
    slots, nodes = nbr_index.shape
    return call(
        count_kernel,
        jax.ShapeDtypeStruct((table_rows, nodes), BF16),
        40e9,
        2 * table_rows * nodes,
        grid=(nodes // QUERY_BLOCK,),
        in_specs=[pl.BlockSpec((slots, QUERY_BLOCK), lambda j: (0, j))],
        out_specs=pl.BlockSpec((table_rows, QUERY_BLOCK), lambda j: (0, j)),
    )(nbr_index)


def encode_kernel(
    head_size, mesh_ref, sum_ref, w_out_ref, gain_ref, w_query_ref, w_key_ref, w_value_ref,
    offer_ref, encoded_ref, query_ref, key_value_ref, offered_ref, acc_ref,
):
    step = pl.program_id(0)
    width = w_value_ref.shape[1]
    head = lax.axis_index("chan") * width // head_size
    columns = pl.ds(pl.multiple_of(head * head_size, head_size), head_size)
    encoded = mesh_ref[...].astype(F32) + contract0(w_out_ref[...], sum_ref[...])
    encoded_ref[...] = encoded
    average = jnp.mean(encoded, axis=0, keepdims=True)
    centred = encoded - average
    variance = jnp.mean(centred * centred, axis=0, keepdims=True)
    normed = (centred * lax.rsqrt(variance + 1e-05) * gain_ref[...]).astype(BF16)
    query_ref[...] = contract0(w_query_ref[:, columns], normed).astype(BF16)
    key = contract0(w_key_ref[:, columns], normed).astype(BF16)
    value = contract0(w_value_ref[...], normed).astype(BF16)
    key_value_ref[:head_size] = key
    key_value_ref[head_size:] = value
    hot = one_hot(step * NODE_BLOCK, NODE_BLOCK, offer_ref[...])

    @pl.when(step == 0)
    def _():
        acc_ref[...] = jnp.zeros_like(acc_ref)

    acc_ref[:head_size] += jnp.dot(key, hot, preferred_element_type=F32)
    acc_ref[head_size:] += jnp.dot(value, hot, preferred_element_type=F32)

    @pl.when(step == pl.num_programs(0) - 1)
    def _():
        offered_ref[...] = acc_ref[...].astype(BF16)


def encode(mesh_latent, node_sum, w_edge_out, gain, w_query, w_key, w_value, offer):
    model_width, nodes = mesh_latent.shape
    hidden = node_sum.shape[0]
    width = w_value.shape[1]
    head_size = model_width // HEADS
    both = head_size + width
    offers = offer.shape[1]
    whole = lambda shape: pl.BlockSpec(shape, lambda j: (0,) * len(shape))
    block = lambda rows: pl.BlockSpec((rows, NODE_BLOCK), lambda j: (0, j))
    return call(
        functools.partial(encode_kernel, head_size),
        [
            jax.ShapeDtypeStruct((model_width, nodes), F32),
            jax.ShapeDtypeStruct((head_size, nodes), BF16),
            jax.ShapeDtypeStruct((both, nodes), BF16),
            jax.ShapeDtypeStruct((both, offers), BF16),
        ],
        2 * model_width * nodes * (hidden + both + head_size),
        10 * mesh_latent.size,
        grid=(nodes // NODE_BLOCK,),
        in_specs=[
            block(model_width),
            block(hidden),
            whole(w_edge_out.shape),
            whole(gain.shape),
            whole(w_query.shape),
            whole(w_key.shape),
            whole(w_value.shape),
            whole(offer.shape),
        ],
        out_specs=[block(model_width), block(head_size), block(both), whole((both, offers))],
        scratch_shapes=[VMEM((both, offers), F32)],
    )(mesh_latent, node_sum, w_edge_out, gain, w_query, w_key, w_value, offer)


def attend_kernel(
    query_ref, own_ref, lower_ref, upper_ref, count_ref, out_ref, key_ref, value_ref
):
    head_size = query_ref.shape[0]

    @pl.when(pl.program_id(0) == 0)
    def _():
        first = 0
        for part in (own_ref, lower_ref, upper_ref):
            rows = part.shape[1]
            key_ref[first : first + rows, :] = part[:head_size].T
            value_ref[:, first : first + rows] = part[head_size:]
            first += rows

    scores = jnp.dot(key_ref[...], query_ref[...], preferred_element_type=F32)
    scores = scores * (head_size**-0.5)
    count = count_ref[...].astype(F32)
    scores = jnp.where(count > 0.0, scores, -3e38)
    top = jnp.max(scores, axis=0, keepdims=True)
    weight = jnp.where(count > 0.0, jnp.exp(scores - top), 0.0)
    total = jnp.sum(weight * count, axis=0, keepdims=True)
    attention = (weight * (1.0 / total)).astype(BF16) * count_ref[...]
    out_ref[...] = jnp.dot(value_ref[...], attention, preferred_element_type=F32).astype(BF16)


def attend(query, own, lower, upper, count):
    head_size, nodes = query.shape
    width = own.shape[0] - head_size
    rows = count.shape[0]
    whole = lambda shape: pl.BlockSpec(shape, lambda j: (0,) * len(shape))
    block = lambda rows: pl.BlockSpec((rows, QUERY_BLOCK), lambda j: (0, j))
    return call(
        attend_kernel,
        jax.ShapeDtypeStruct((width, nodes), BF16),
        2 * nodes * rows * (head_size + width),
        2 * count.size,
        grid=(nodes // QUERY_BLOCK,),
        in_specs=[
            block(head_size),
            whole(own.shape),
            whole(lower.shape),
            whole(upper.shape),
            block(rows),
        ],
        out_specs=block(width),
        scratch_shapes=[VMEM((rows, head_size), BF16), VMEM((width, rows), BF16)],
    )(query, own, lower, upper, count)


def output_kernel(encoded_ref, blended_ref, weight_ref, out_ref):
    out_ref[...] = (encoded_ref[...] + contract0(weight_ref[...], blended_ref[...])).astype(BF16)


def output(encoded, blended, weight):
    model_width, nodes = encoded.shape
    block = lambda rows: pl.BlockSpec((rows, NODE_BLOCK), lambda j: (0, j))
    return call(
        output_kernel,
        jax.ShapeDtypeStruct((model_width, nodes), BF16),
        2 * weight.size * nodes,
        8 * encoded.size,
        grid=(nodes // NODE_BLOCK,),
        in_specs=[
            block(model_width),
            block(blended.shape[0]),
            pl.BlockSpec(weight.shape, lambda j: (0, 0)),
        ],
        out_specs=block(model_width),
    )(encoded, blended, weight)


def per_device(
    grid_latent,
    mesh_latent,
    edge_sender,
    edge_receiver,
    edge_count,
    nbr_index,
    halo_send,
    w_edge_send,
    w_edge_recv,
    b_edge,
    w_edge_out,
    ln_gain,
    w_query,
    w_key,
    w_value,
    w_attn_out,
):
    patch_pos = lax.axis_index("patch")
    patches = lax.axis_size("patch")
    nodes = mesh_latent.shape[1]
    capacity = edge_sender.shape[2]
    halo_rows = halo_send.shape[2]
    counts_in = jnp.take(edge_count, patch_pos, axis=1)
    usable = jnp.arange(capacity, dtype=jnp.int32)[None, :] < counts_in[:, None]
    target = jnp.where(usable, edge_receiver[:, 0, :], -1)

    w_edge_out_all = lax.all_gather(w_edge_out, "chan", axis=0, tiled=True)
    w_attn_out_all = lax.all_gather(w_attn_out, "chan", axis=0, tiled=True)

    outgoing = project_pick(grid_latent, w_edge_send, edge_sender[0])
    sent = lax.all_to_all(outgoing, "patch", split_axis=0, concat_axis=0, tiled=True)
    received = project_pick(mesh_latent, w_edge_recv, target)
    node_sum = edge_sum(sent, received, b_edge[:, None], target, nodes)
    node_sum_all = lax.all_gather(node_sum, "chan", axis=0, tiled=True)
    count = count_slots(nbr_index, nodes + 2 * halo_rows)
    encoded, query, key_value, offered = encode(
        mesh_latent, node_sum_all, w_edge_out_all, ln_gain[:, None],
        w_query, w_key, w_value, halo_send.reshape(1, -1),
    )
    up = [(i, (i + 1) % patches) for i in range(patches)]
    down = [((i + 1) % patches, i) for i in range(patches)]
    lower = lax.ppermute(offered[:, halo_rows:], "patch", up)
    upper = lax.ppermute(offered[:, :halo_rows], "patch", down)
    blended = attend(query, key_value, lower, upper, count)
    blended_all = lax.all_gather(blended, "chan", axis=0, tiled=True)
    return output(encoded, blended_all, w_attn_out_all)


def solution(mesh):
    in_specs = (
        P("member", "patch"),
        P("member", "patch"),
        P("patch", None, None),
        P(None, "patch", None),
        P(),
        P(None, "patch"),
        P("patch", None, None),
        P(None, "chan"),
        P(None, "chan"),
        P("chan"),
        P("chan", None),
        P(),
        P(),
        P(),
        P(None, "chan"),
        P("chan", None),
    )
    out_specs = P("member", "patch")
    return jax.shard_map(
        per_device, mesh=mesh, in_specs=in_specs, out_specs=out_specs, check_vma=False
    )
```

time: 640 us -> 176 us (0.28)
  local copies, waits for them, and re-layouts: 224 us -> 14.1 us
  waiting for transfers between devices: 246 us -> 48.6 us
  other arithmetic: 82.3 us -> 0.26 us
  matrix products: 60.4 us -> 0 us
  Pallas kernels: 0 us -> 51.5 us
  blocking collectives: 0 us -> 41.5 us
    psum x2 -> x0, waiting for transfers between devices: 242 us -> none  [the longest x1 122 us: per_device(): lax.psum(contract(w_edge_out, node_sum), 'chan')]
    gather x7 -> x0, local copies, waits for them, and re-layouts: 130 us -> none  [the longest x3 103 us: attend(): picked = jnp.take(key_table, chosen, axis=0)]
    dot_general x13 -> x0, matrix products: 60.4 us -> none  [the longest x3 39.7 us: attend(): jnp.einsum('bhd,kbhd->hkb', query_block, key_block, preferred_element_typ...]
    pallas_call x0 -> x7, Pallas kernels: none -> 51.5 us  [the longest x1 19.6 us: count_slots(): call(count_kernel, jax.ShapeDtypeStruct((table_rows, nodes), BF16), 40000...]
    all_gather x0 -> x2, blocking collectives: none -> 41.5 us  [the longest x1 21.6 us: per_device(): w_edge_out_all = lax.all_gather(w_edge_out, 'chan', axis=0, tiled=True)]
    reshape x6 -> x0, local copies, waits for them, and re-layouts: 40.4 us -> none  [the longest x3 37.6 us: attend(): picked[:, :model_width].reshape(neighbours, block_rows, HEADS, head_size)]
    all_gather x0 -> x2, waiting for transfers between devices: none -> 38.3 us  [the longest x1 19.4 us: per_device(): node_sum_all = lax.all_gather(node_sum, 'chan', axis=0, tiled=True)]
    select_n x13 -> x1, other arithmetic: 38.3 us -> 0.07 us  [per_device(): target = jnp.where(usable, edge_receiver[:, 0, :], -1)]
  transfers between devices with their start and end apart: 5 -> 5, of which waited for: 5 -> 3; matrix products, arithmetic and copies ran while one was open for 3% -> 0% of each run, Pallas kernels for 0% -> 13%
where the time goes in v1:
time: 176 us
  Pallas kernels  51.5 us (29%)
  waiting for transfers between devices  48.6 us (28%)
  blocking collectives  41.5 us (24%)
  local copies, waits for them, and re-layouts  14.1 us (8%)
  between operations  13.5 us (8%)
  starting transfers between devices  6.19 us (4%)
    all_gather x1, blocking collectives, per_device(): w_edge_out_all = lax.all_gather(w_edge_out, 'chan', axis=0, tiled=True)  21.6 us
    all_gather x1, blocking collectives, per_device(): w_attn_out_all = lax.all_gather(w_attn_out, 'chan', axis=0, tiled=True)  19.9 us
    pallas_call x1, Pallas kernels, count_slots(): call(count_kernel, jax.ShapeDtypeStruct((table_rows, nodes), BF16), 40000...  19.6 us
    all_gather x1, waiting for transfers between devices, per_device(): node_sum_all = lax.all_gather(node_sum, 'chan', axis=0, tiled=True)  19.4 us
    all_gather x1, waiting for transfers between devices, per_device(): blended_all = lax.all_gather(blended, 'chan', axis=0, tiled=True)  18.9 us
    unnamed x46, local copies, waits for them, and re-layouts  13.8 us
    pallas_call x1, Pallas kernels, attend(): call(attend_kernel, jax.ShapeDtypeStruct((width, nodes), BF16), 2 * nodes...  11.4 us
    all_to_all x1, waiting for transfers between devices, per_device(): lax.all_to_all(outgoing, 'patch', split_axis=0, concat_axis=0, tiled=True)  10.3 us
  transfers between devices with their start and end apart: 5, of which 3 were waited for; matrix products, arithmetic and copies ran while one was open for 0% of the time, Pallas kernels for 13%

profile of v1, /device:TPU:0, one launch (start us, length us, event | category | flops | bytes accessed | tf_op | source)
XLA Modules:
  0.0 175.7 jit_solution(4902179838135723726)
XLA Ops:
  6.5 1.6 copy-done.3
  8.1 0.9 copy-done.9
  9.0 0.7 copy-done.13
  9.7 4.1 %shard_map.154 = bf16[4,128,1024]{2,1,0:T(8,128)(2,1)} custom-call(bf16[512,2048]{1,0:T(8,128)(2,1)S(1)} %copy-done.3, bf16[512,128]{1,0:T(8,128)(2,1)S(1)} %copy-done.9, s32[4,1024]{1,0:T(4,128)S(1)} %bitcast.6), custom_call_target="tpu_custom_call" | custom-call | flops 2415919104 | bytes 3276800 | tf_op jit(solution)/shard_map/pallas_call | solution.py:69
  13.9 0.0 copy-start.10
  13.9 4.4 %all-to-all-start = ((bf16[4,128,1024]{2,1,0:T(8,128)(2,1)}), bf16[4,128,1024]{2,1,0:T(8,128)(2,1)S(1)}, u32[]{:S(2)}, u32[]{:S(2)}) async-start(bf16[4,128,1024]{2,1,0:T(8,128)(2,1)} %shard_map.154), calls=%async_computation | async-start | bytes 2097152 | tf_op jit(solution)/shard_map/all_to_all | solution.py:322
  18.2 0.0 all-gather.3.cloned.1.call-start
  18.2 0.0 copy-done.22
  18.2 0.1 copy.18.bias_ref
  18.3 0.0 copy-done.21
  18.3 0.2 select_reduce_fusion
  18.5 0.0 copy-done.19
  18.5 0.1 bitcast_select_fusion.index_ref
  18.6 0.0 copy-done.4
  18.6 0.0 copy-done.10
  18.6 2.8 %shard_map.155.received_ref = bf16[4,128,1024]{2,1,0:T(8,128)(2,1)S(1)} custom-call(bf16[512,1536]{1,0:T(8,128)(2,1)S(1)} %copy-done.4, bf16[512,128]{1,0:T(8,128)(2,1)S(1)} %copy-done.10, s32[4,1024]{1,0:T(4,128)S(1)} %bitcast_select_fusion.index_ref), custom_call_target="tpu_custom_call" | custom-call | flops 1811939328 | bytes 2752512 | tf_op jit(solution)/shard_map/pallas_call | solution.py:69
  21.4 0.0 copy-start.15
  21.4 1.0 copy-done.15
  22.4 10.3 %all-to-all-done.sent_ref = bf16[4,128,1024]{2,1,0:T(8,128)(2,1)S(1)} async-done(((bf16[4,128,1024]{2,1,0:T(8,128)(2,1)}), bf16[4,128,1024]{2,1,0:T(8,128)(2,1)S(1)}, u32[]{:S(2)}, u32[]{:S(2)}) %all-to-all-start) | async-done | bytes 1048608 | tf_op jit(solution)/shard_map/all_to_all | solution.py:322
  32.7 1.2 copy-done.16
  33.9 6.4 %shard_map.156 = bf16[128,1536]{1,0:T(8,128)(2,1)} custom-call(bf16[4,128,1024]{2,1,0:T(8,128)(2,1)S(1)} %all-to-all-done.sent_ref, bf16[4,128,1024]{2,1,0:T(8,128)(2,1)S(1)} %copy-done.16, f32[128,1]{1,0:T(8,128)S(1)} %copy.18.bias_ref, s32[4,1024]{1,0:T(4,128)S(1)} %bitcast_select_fusion.index_ref), custom_call_target="tpu_custom_call" | custom-call | flops 1610612736 | bytes 2097152 | tf_op jit(solution)/shard_map/pallas_call | solution.py:109
  40.4 0.0 all-gather.3.cloned.1.call-update
  40.4 0.0 all-gather.5.cloned.1.call-start
  40.4 0.0 copy-done.20
  40.4 0.1 copy.19.gain_ref
  40.6 0.0 copy-done.17
  40.6 21.6 %all_gather.13.w_out_ref = bf16[512,512]{1,0:T(8,128)(2,1)} all-gather(bf16[128,512]{1,0:T(8,128)(2,1)S(1)} %copy-done.17), channel_id=1, replica_groups=mesh['member'=2,'patch'=4,'chan'=4] {'chan'}, dimensions={0}, use_global_device_ids=true | all-gather | bytes 655360 | tf_op jit(solution)/shard_map/all_gather | solution.py:318
  62.2 19.4 %all-gather.3.cloned.1.call-done.sum_ref = bf16[512,1536]{1,0:T(8,128)(2,1)} async-done(((bf16[128,1536]{1,0:T(8,128)(2,1)}), bf16[512,1536]{1,0:T(8,128)(2,1)}) %all-gather.3.cloned.1.call-update) | async-done | bytes 1572880 | tf_op jit(solution)/shard_map/all_gather | solution.py:325
  81.6 0.0 copy-done.14
  81.6 1.0 copy-done.2
  82.7 1.4 copy-done.5
  84.1 1.4 copy-done.6
  85.5 1.0 copy-done.7
  86.6 1.0 copy-done.8
  87.6 4.5 %shard_map.157 = (f32[512,1536]{1,0:T(8,128)S(1)}, bf16[128,1536]{1,0:T(8,128)(2,1)S(1)}, bf16[256,1536]{1,0:T(8,128)(2,1)S(1)}, bf16[256,256]{1,0:T(8,128)(2,1)S(1)}) custom-call(bf16[512,1536]{1,0:T(8,128)(2,1)S(1)} %copy-done.5, bf16[512,1536]{1,0:T(8,128)(2,1)S(1)} %copy-done.6, bf16[512,512]{1,0:T(8,128)(2,1)S(1)} %copy-done.2, ...), custom_call_target="tpu_custom_call" | custom-call | flops 1409286144 | bytes 7864320 | tf_op jit(solution)/shard_map/pallas_call | solution.py:194
  92.1 0.1 collective-permute-start
  92.2 1.7 collective-permute-start.1
  93.9 19.6 %shard_map.158.count_ref = bf16[1792,1536]{1,0:T(8,128)(2,1)S(1)} custom-call(s32[16,1536]{1,0:T(8,128)S(1)} %copy-done.12), custom_call_target="tpu_custom_call" | custom-call | flops 40000000000 | bytes 5505024 | tf_op jit(solution)/shard_map/pallas_call | solution.py:141
  113.5 0.0 collective-permute-done.lower_ref
  113.5 0.0 collective-permute-done.1.upper_ref
  113.5 0.0 copy-start.18
  113.5 11.4 %shard_map.159 = bf16[128,1536]{1,0:T(8,128)(2,1)} custom-call(bf16[128,1536]{1,0:T(8,128)(2,1)S(1)} %get-tuple-element.10.query_ref, bf16[256,1536]{1,0:T(8,128)(2,1)S(1)} %get-tuple-element.11.own_ref, bf16[256,128]{1,0:T(8,128)(2,1)S(1)} %collective-permute-done.lower_ref, bf16[256,128]{1,0:T(8,128)(2,1)S(1)} %collective-permute-done.1.upper_ref, ...), custom_call_target="tpu_custom_call" | custom-call | flops 1409286144 | bytes 5505024 | tf_op jit(solution)/shard_map/pallas_call | solution.py:251
  124.9 0.0 all-gather.5.cloned.1.call-update
  124.9 19.9 %all_gather.15.weight_ref = bf16[512,512]{1,0:T(8,128)(2,1)} all-gather(bf16[128,512]{1,0:T(8,128)(2,1)S(1)} %copy-done.18), channel_id=1, replica_groups=mesh['member'=2,'patch'=4,'chan'=4] {'chan'}, dimensions={0}, use_global_device_ids=true | all-gather | bytes 655360 | tf_op jit(solution)/shard_map/all_gather | solution.py:319
  144.8 18.9 %all-gather.5.cloned.1.call-done.blended_ref = bf16[512,1536]{1,0:T(8,128)(2,1)} async-done(((bf16[128,1536]{1,0:T(8,128)(2,1)}), bf16[512,1536]{1,0:T(8,128)(2,1)}) %all-gather.5.cloned.1.call-update) | async-done | bytes 1572880 | tf_op jit(solution)/shard_map/all_gather | solution.py:336
  163.7 1.0 copy-done
  164.7 1.4 copy-done.1
  166.1 2.8 %shard_map.160 = bf16[512,1536]{1,0:T(8,128)(2,1)} custom-call(f32[512,1536]{1,0:T(8,128)S(1)} %get-tuple-element.9.encoded_ref, bf16[512,1536]{1,0:T(8,128)(2,1)S(1)} %copy-done.1, bf16[512,512]{1,0:T(8,128)(2,1)S(1)} %copy-done), custom_call_target="tpu_custom_call" | custom-call | flops 805306368 | bytes 6291456 | tf_op jit(solution)/shard_map/pallas_call | solution.py:276
  (24 shorter events, 0.0 us)
Async XLA Ops:
  6.5 1.6 copy-start.3
  8.1 0.9 copy-start.9
  9.0 0.7 copy-start.13
  13.8 4.4 %copy-start.22 = (f32[128]{0:T(128)S(1)}, f32[128]{0:T(128)}, u32[]{:S(2)}) copy-start(f32[128]{0:T(128)} %param.25) | copy-start | bytes 1540
  13.8 4.5 %copy-start.21 = (s32[4,4]{1,0:T(4,128)S(1)}, s32[4,4]{1,0:T(4,128)}, u32[]{:S(2)}) copy-start(s32[4,4]{1,0:T(4,128)} %param.20) | copy-start | bytes 196
  13.8 4.7 %copy-start.19 = (s32[4,1,1024]{2,1,0:T(1,128)S(1)}, s32[4,1,1024]{2,1,0:T(1,128)}, u32[]{:S(2)}) copy-start(s32[4,1,1024]{2,1,0:T(1,128)} %param.19) | copy-start | bytes 49156
  13.9 4.8 %copy-start.4 = (bf16[512,1536]{1,0:T(8,128)(2,1)S(1)}, bf16[512,1536]{1,0:T(8,128)(2,1)}, u32[]{:S(2)}) copy-start(bf16[512,1536]{1,0:T(8,128)(2,1)} %mesh_ref.1) | copy-start | bytes 4718596
  13.9 4.8 %copy-start.10 = (bf16[512,128]{1,0:T(8,128)(2,1)S(1)}, bf16[512,128]{1,0:T(8,128)(2,1)}, u32[]{:S(2)}) copy-start(bf16[512,128]{1,0:T(8,128)(2,1)} %weight_ref.3) | copy-start | bytes 393220
  13.9 18.8 %all-to-all-start = ((bf16[4,128,1024]{2,1,0:T(8,128)(2,1)}), bf16[4,128,1024]{2,1,0:T(8,128)(2,1)S(1)}, u32[]{:S(2)}, u32[]{:S(2)}) async-start(bf16[4,128,1024]{2,1,0:T(8,128)(2,1)} %shard_map.154), calls=%async_computation | async-start | bytes 2097152 | tf_op jit(solution)/shard_map/all_to_all | solution.py:322
  18.2 63.4 %all-gather.3.cloned.1.call-start = ((), (), s32[]{:S(2)}) async-start(), calls=%async_computation.1 | async-start | bytes 1966080 | tf_op jit(solution)/shard_map/all_gather | solution.py:325
  21.4 1.0 copy-start.15
  22.4 59.3 %copy-start.11 = (bf16[512,128]{1,0:T(8,128)(2,1)S(1)}, bf16[512,128]{1,0:T(8,128)(2,1)}, u32[]{:S(2)}) copy-start(bf16[512,128]{1,0:T(8,128)(2,1)} %w_value_ref.1) | copy-start | bytes 393220
  22.4 59.3 %copy-start.14 = (s32[1,2,128]{2,1,0:T(2,128)S(1)}, s32[1,2,128]{2,1,0:T(2,128)}, u32[]{:S(2)}) copy-start(s32[1,2,128]{2,1,0:T(2,128)} %param.22) | copy-start | bytes 3076
  32.7 1.2 copy-start.16
  33.9 6.5 %copy-start.20 = (f32[512]{0:T(512)S(1)}, f32[512]{0:T(512)}, u32[]{:S(2)}) copy-start(f32[512]{0:T(512)} %param.27) | copy-start | bytes 6148
  33.9 6.7 %copy-start.17 = (bf16[128,512]{1,0:T(8,128)(2,1)S(1)}, bf16[128,512]{1,0:T(8,128)(2,1)}, u32[]{:S(2)}) copy-start(bf16[128,512]{1,0:T(8,128)(2,1)} %param.26) | copy-start | bytes 393220
  40.4 123.3 %all-gather.5.cloned.1.call-start = ((), (), s32[]{:S(2)}) async-start(), calls=%async_computation.2 | async-start | bytes 1966080 | tf_op jit(solution)/shard_map/all_gather | solution.py:336
  81.6 1.0 copy-start.2
  82.7 1.4 copy-start.5
  84.1 1.4 copy-start.6
  85.5 1.0 copy-start.7
  86.5 1.0 copy-start.8
  87.6 6.3 %copy-start.12 = (s32[16,1536]{1,0:T(8,128)S(1)}, s32[16,1536]{1,0:T(8,128)}, u32[]{:S(2)}) copy-start(s32[16,1536]{1,0:T(8,128)} %index_ref.1) | copy-start | bytes 294916
  92.1 21.4 %collective-permute-start = (bf16[256,128]{1,0:T(8,128)(2,1)S(1)}, bf16[256,128]{1,0:T(8,128)(2,1)S(1)}, u32[]{:S(2)}, u32[]{:S(2)}) collective-permute-start(bf16[256,128]{1,0:T(8,128)(2,1)S(1)} %get-tuple-element.25), channel_id=1, source_target_pairs={{0,4},{4,8},{8,12},{12,0},{1,5},{5,9},{9,13},{13,1},{2,6},{6,10},{... | collective-permute-start | bytes 196616 | tf_op jit(solution)/shard_map/ppermute | solution.py:333
  92.2 21.3 %collective-permute-start.1 = (bf16[256,128]{1,0:T(8,128)(2,1)S(1)}, bf16[256,128]{1,0:T(8,128)(2,1)S(1)}, u32[]{:S(2)}, u32[]{:S(2)}) collective-permute-start(bf16[256,128]{1,0:T(8,128)(2,1)S(1)} %get-tuple-element.24), channel_id=1, source_target_pairs={{4,0},{8,4},{12,8},{0,12},{5,1},{9,5},{13,9},{1,13},{6,2},{10,6},{... | collective-permute-start | bytes 196616 | tf_op jit(solution)/shard_map/ppermute | solution.py:334
  113.5 11.4 %copy-start.18 = (bf16[128,512]{1,0:T(8,128)(2,1)S(1)}, bf16[128,512]{1,0:T(8,128)(2,1)}, u32[]{:S(2)}) copy-start(bf16[128,512]{1,0:T(8,128)(2,1)} %param.31) | copy-start | bytes 393220
  163.7 1.0 copy-start
  164.7 1.4 copy-start.1
Sparse Core Ops, SparseCore 0:
  40.5 41.0 all-gather.2
  125.0 38.5 all-gather.4

commit v2 on v0

v2 whole, which is shorter than its diff:
```python
import functools

import jax
import jax.numpy as jnp
from jax import lax
from jax.experimental import pallas as pl
from jax.experimental.pallas import tpu as pltpu
from jax.sharding import PartitionSpec as P

HEADS = 4
BF16 = jnp.bfloat16
F32 = jnp.float32
VMEM = pltpu.VMEM
QUERY_BLOCK = 256
NODE_BLOCK = 512
ONEHOT_ROWS = 256
COUNT_ROWS = 64


def contract0(weight, operand):
    return lax.dot_general(
        weight, operand, (((0,), (0,)), ((), ())), preferred_element_type=F32
    )


def one_hot(first, rows, index_row):
    shape = (rows, index_row.shape[1])
    ids = lax.broadcasted_iota(jnp.int32, shape, 0)
    return jnp.where(ids == index_row - first, 1.0, 0.0).astype(BF16)


def pick_columns(table_ref, index_row):
    picked = None
    for first in range(0, table_ref.shape[1], ONEHOT_ROWS):
        term = jnp.dot(
            table_ref[:, first : first + ONEHOT_ROWS],
            one_hot(first, ONEHOT_ROWS, index_row),
            preferred_element_type=F32,
        )
        picked = term if picked is None else picked + term
    return picked


def kernel(
    patches, chans,
    grid_ref, mesh_ref, sender_ref, target_ref, nbr_ref, offer_ref,
    w_send_ref, w_recv_ref, bias_ref, w_edge_out_ref, gain_ref, w_query_ref, w_key_ref,
    w_value_ref, w_attn_out_ref,
    out_ref,
    sender_table, recv_table, send_buf, recv_buf, received, acc, sums_mine, sums,
    w_edge_out, w_attn_out, encoded, query, key, value, offered_acc, offered, halo, count,
    blended_mine, blended,
    weight_send, weight_recv, edge_send, edge_recv, sum_send, sum_recv, halo_send, halo_recv,
    blend_send, blend_recv,
):
    patch = lax.axis_index("patch")
    chan = lax.axis_index("chan")
    nodes = mesh_ref.shape[1]
    width = w_value_ref.shape[1]
    head_size = query.shape[0]
    node_blocks = nodes // NODE_BLOCK
    query_blocks = nodes // QUERY_BLOCK
    halo_rows = halo.shape[2]

    barrier = pltpu.get_barrier_semaphore()
    for off in range(1, chans):
        pl.semaphore_signal(
            barrier, inc=1, device_id={"chan": lax.rem(chan + off, chans)},
            device_id_type=pl.DeviceIdType.MESH,
        )
    for off in range(1, patches):
        pl.semaphore_signal(
            barrier, inc=1, device_id={"patch": lax.rem(patch + off, patches)},
            device_id_type=pl.DeviceIdType.MESH,
        )
    pl.semaphore_wait(barrier, chans + patches - 2)

    def to_chans(source, target, send_sems, recv_sems):
        return [
            pltpu.make_async_remote_copy(
                src_ref=source, dst_ref=target,
                send_sem=send_sems.at[off - 1], recv_sem=recv_sems.at[off - 1],
                device_id={"chan": lax.rem(chan + off, chans)},
                device_id_type=pl.DeviceIdType.MESH,
            )
            for off in range(1, chans)
        ]

    pending = []

    def start(copies):
        for copy in copies:
            copy.start()
        pending.extend(copies)
        return copies

    edge_out_copies = start(
        to_chans(w_edge_out_ref, w_edge_out.at[chan], weight_send.at[0], weight_recv.at[0])
    )
    w_edge_out[chan] = w_edge_out_ref[...]
    w_attn_out[chan] = w_attn_out_ref[...]

    sender_table[...] = contract0(w_send_ref[...], grid_ref[...]).astype(BF16)
    offs = sorted(range(1, patches), key=lambda off: -min(off, patches - off))
    edge_copies = {}
    for off in offs:
        other = lax.rem(patch + off, patches)
        send_buf[off] = pick_columns(sender_table, sender_ref[pl.ds(other, 1), :]).astype(BF16)
        edge_copies[off] = pltpu.make_async_remote_copy(
            src_ref=send_buf.at[off], dst_ref=recv_buf.at[off],
            send_sem=edge_send.at[off], recv_sem=edge_recv.at[off],
            device_id={"patch": other}, device_id_type=pl.DeviceIdType.MESH,
        )
        start([edge_copies[off]])
    attn_out_copies = start(
        to_chans(w_attn_out_ref, w_attn_out.at[chan], weight_send.at[1], weight_recv.at[1])
    )
    recv_buf[0] = pick_columns(sender_table, sender_ref[pl.ds(patch, 1), :]).astype(BF16)

    recv_table[...] = contract0(w_recv_ref[...], mesh_ref[...]).astype(BF16)
    order = [0] + offs
    for off in order:
        band = lax.rem(patch + patches - off, patches)
        received[off] = pick_columns(recv_table, target_ref[pl.ds(band, 1), :]).astype(BF16)
    for place, off in enumerate(order):
        if off:
            edge_copies[off].wait_recv()
        band = lax.rem(patch + patches - off, patches)
        index_row = target_ref[pl.ds(band, 1), :]
        summed = recv_buf[off].astype(F32) + received[off].astype(F32) + bias_ref[...]
        hidden = (summed / (1.0 + jnp.exp(-summed))).astype(BF16)
        for first in range(0, nodes, ONEHOT_ROWS):
            columns = slice(first, first + ONEHOT_ROWS)
            term = lax.dot_general(
                hidden, one_hot(first, ONEHOT_ROWS, index_row),
                (((1,), (1,)), ((), ())), preferred_element_type=F32,
            )
            if place:
                term += acc[:, columns]
            acc[:, columns] = term

    sum_copies = []
    for block in range(node_blocks):
        node_sum = acc[:, block * NODE_BLOCK : (block + 1) * NODE_BLOCK].astype(BF16)
        sums_mine[block] = node_sum
        sum_copies.append(
            start(
                to_chans(
                    sums_mine.at[block], sums.at[block, chan],
                    sum_send.at[block], sum_recv.at[block],
                )
            )
        )
        sums[block, chan] = node_sum

    def count_block(block):
        index = nbr_ref[:, block * QUERY_BLOCK : (block + 1) * QUERY_BLOCK]
        ids = lax.broadcasted_iota(jnp.int32, (COUNT_ROWS, QUERY_BLOCK), 0)

        def body(step, carry):
            first = step * COUNT_ROWS
            here = ids + first
            total = jnp.zeros((COUNT_ROWS, QUERY_BLOCK), F32)
            for slot in range(index.shape[0]):
                total += jnp.where(here == index[slot : slot + 1, :], 1.0, 0.0)
            rows = pl.ds(pl.multiple_of(first, COUNT_ROWS), COUNT_ROWS)
            count[block, rows, :] = total.astype(BF16)
            return carry

        lax.fori_loop(0, count.shape[1] // COUNT_ROWS, body, 0)

    for block in range(query_blocks - 1):
        count_block(block)

    for copy in edge_out_copies:
        copy.wait_recv()
    head = chan * width // head_size
    columns = pl.ds(pl.multiple_of(head * head_size, head_size), head_size)
    for block in range(node_blocks):
        for copy in sum_copies[block]:
            copy.wait_recv()
        here = slice(block * NODE_BLOCK, (block + 1) * NODE_BLOCK)
        hidden_units = chans * w_edge_out.shape[1]
        weight = w_edge_out[...].reshape(hidden_units, -1)
        node_sum = sums[block].reshape(hidden_units, -1)
        enc = mesh_ref[:, here].astype(F32) + contract0(weight, node_sum)
        encoded[:, here] = enc
        average = jnp.mean(enc, axis=0, keepdims=True)
        centred = enc - average
        variance = jnp.mean(centred * centred, axis=0, keepdims=True)
        normed = (centred * lax.rsqrt(variance + 1e-05) * gain_ref[...]).astype(BF16)
        query[:, here] = contract0(w_query_ref[:, columns], normed).astype(BF16)
        block_key = contract0(w_key_ref[:, columns], normed).astype(BF16)
        block_value = contract0(w_value_ref[...], normed).astype(BF16)
        key[here, :] = block_key.T
        value[:, here] = block_value
        hot = one_hot(block * NODE_BLOCK, NODE_BLOCK, offer_ref[...])
        key_term = jnp.dot(block_key, hot, preferred_element_type=F32)
        value_term = jnp.dot(block_value, hot, preferred_element_type=F32)
        if block:
            key_term += offered_acc[:head_size]
            value_term += offered_acc[head_size:]
        offered_acc[:head_size] = key_term
        offered_acc[head_size:] = value_term

    halo_copies = []
    for side in range(2):
        offered[side] = offered_acc[:, side * halo_rows : (side + 1) * halo_rows].astype(BF16)
        step = 1 if side == 1 else patches - 1
        halo_copies.append(
            pltpu.make_async_remote_copy(
                src_ref=offered.at[side], dst_ref=halo.at[side],
                send_sem=halo_send.at[side], recv_sem=halo_recv.at[side],
                device_id={"patch": lax.rem(patch + step, patches)},
                device_id_type=pl.DeviceIdType.MESH,
            )
        )
    start(halo_copies)
    count_block(query_blocks - 1)
    first = nodes
    for side in (1, 0):
        halo_copies[side].wait_recv()
        key[first : first + halo_rows, :] = halo[side, :head_size].T
        value[:, first : first + halo_rows] = halo[side, head_size:]
        first += halo_rows

    blend_copies = []
    for block in range(query_blocks):
        here = slice(block * QUERY_BLOCK, (block + 1) * QUERY_BLOCK)
        scores = jnp.dot(key[...], query[:, here], preferred_element_type=F32)
        scores = scores * (head_size**-0.5)
        slots = count[block].astype(F32)
        scores = jnp.where(slots > 0.0, scores, -3e38)
        top = jnp.max(scores, axis=0, keepdims=True)
        weight = jnp.where(slots > 0.0, jnp.exp(scores - top), 0.0)
        total = jnp.sum(weight * slots, axis=0, keepdims=True)
        attention = (weight * (1.0 / total)).astype(BF16) * count[block]
        mixed = jnp.dot(value[...], attention, preferred_element_type=F32).astype(BF16)
        blended_mine[block] = mixed
        blend_copies.append(
            start(
                to_chans(
                    blended_mine.at[block], blended.at[block, chan],
                    blend_send.at[block], blend_recv.at[block],
                )
            )
        )
        blended[block, chan] = mixed

    for copy in attn_out_copies:
        copy.wait_recv()
    for block in range(query_blocks):
        for copy in blend_copies[block]:
            copy.wait_recv()
        here = slice(block * QUERY_BLOCK, (block + 1) * QUERY_BLOCK)
        rows = chans * w_attn_out.shape[1]
        weight = w_attn_out[...].reshape(rows, -1)
        update = contract0(weight, blended[block].reshape(rows, -1))
        out_ref[:, here] = (encoded[:, here] + update).astype(BF16)

    for copy in pending:
        copy.wait_send()


def per_device(
    grid_latent,
    mesh_latent,
    edge_sender,
    edge_receiver,
    edge_count,
    nbr_index,
    halo_send,
    w_edge_send,
    w_edge_recv,
    b_edge,
    w_edge_out,
    ln_gain,
    w_query,
    w_key,
    w_value,
    w_attn_out,
):
    patch_pos = lax.axis_index("patch")
    patches = lax.axis_size("patch")
    chans = lax.axis_size("chan")
    model_width, nodes = mesh_latent.shape
    capacity = edge_sender.shape[2]
    halo_rows = halo_send.shape[2]
    hidden = w_edge_send.shape[1]
    width = w_value.shape[1]
    head_size = model_width // HEADS
    both = head_size + width
    table_rows = nodes + 2 * halo_rows
    node_blocks = nodes // NODE_BLOCK
    query_blocks = nodes // QUERY_BLOCK
    counts_in = jnp.take(edge_count, patch_pos, axis=1)
    usable = jnp.arange(capacity, dtype=jnp.int32)[None, :] < counts_in[:, None]
    target = jnp.where(usable, edge_receiver[:, 0, :], -1)
    sem = lambda *shape: pltpu.SemaphoreType.DMA(shape)
    return pl.pallas_call(
        functools.partial(kernel, patches, chans),
        out_shape=jax.ShapeDtypeStruct((model_width, nodes), BF16),
        in_specs=[pl.BlockSpec(memory_space=VMEM)] * 15,
        out_specs=pl.BlockSpec(memory_space=VMEM),
        scratch_shapes=[
            VMEM((hidden, grid_latent.shape[1]), BF16),
            VMEM((hidden, nodes), BF16),
            VMEM((patches, hidden, capacity), BF16),
            VMEM((patches, hidden, capacity), BF16),
            VMEM((patches, hidden, capacity), BF16),
            VMEM((hidden, nodes), F32),
            VMEM((node_blocks, hidden, NODE_BLOCK), BF16),
            VMEM((node_blocks, chans, hidden, NODE_BLOCK), BF16),
            VMEM((chans,) + w_edge_out.shape, BF16),
            VMEM((chans,) + w_attn_out.shape, BF16),
            VMEM((model_width, nodes), F32),
            VMEM((head_size, nodes), BF16),
            VMEM((table_rows, head_size), BF16),
            VMEM((width, table_rows), BF16),
            VMEM((both, 2 * halo_rows), F32),
            VMEM((2, both, halo_rows), BF16),
            VMEM((2, both, halo_rows), BF16),
            VMEM((query_blocks, table_rows, QUERY_BLOCK), BF16),
            VMEM((query_blocks, width, QUERY_BLOCK), BF16),
            VMEM((query_blocks, chans, width, QUERY_BLOCK), BF16),
            sem(2, chans), sem(2, chans),
            sem(patches), sem(patches),
            sem(node_blocks, chans), sem(node_blocks, chans),
            sem(2), sem(2),
            sem(query_blocks, chans), sem(query_blocks, chans),
        ],
        compiler_params=pltpu.CompilerParams(
            collective_id=0, has_side_effects=True, vmem_limit_bytes=56 * 2**20
        ),
    )(
        grid_latent, mesh_latent, edge_sender[0], target, nbr_index,
        halo_send.reshape(1, -1), w_edge_send, w_edge_recv, b_edge[:, None], w_edge_out,
        ln_gain[:, None], w_query, w_key, w_value, w_attn_out,
    )


def solution(mesh):
    in_specs = (
        P("member", "patch"),
        P("member", "patch"),
        P("patch", None, None),
        P(None, "patch", None),
        P(),
        P(None, "patch"),
        P("patch", None, None),
        P(None, "chan"),
        P(None, "chan"),
        P("chan"),
        P("chan", None),
        P(),
        P(),
        P(),
        P(None, "chan"),
        P("chan", None),
    )
    out_specs = P("member", "patch")
    return jax.shard_map(
        per_device, mesh=mesh, in_specs=in_specs, out_specs=out_specs, check_vma=False
    )
```

time: 640 us -> 115 us (0.18)
  waiting for transfers between devices: 246 us -> 0 us
  local copies, waits for them, and re-layouts: 224 us -> 5.56 us
  Pallas kernels: 0 us -> 107 us
  other arithmetic: 82.3 us -> 2.26 us
  matrix products: 60.4 us -> 0 us
  between operations: 13.8 us -> 0.01 us
    psum x2 -> x0, waiting for transfers between devices: 242 us -> none  [the longest x1 122 us: per_device(): lax.psum(contract(w_edge_out, node_sum), 'chan')]
    gather x7 -> x0, local copies, waits for them, and re-layouts: 130 us -> none  [the longest x3 103 us: attend(): picked = jnp.take(key_table, chosen, axis=0)]
    pallas_call x0 -> x1, Pallas kernels: none -> 107 us  [per_device(): pl.pallas_call(functools.partial(kernel, patches, chans), out_shape=jax.S...]
    dot_general x13 -> x0, matrix products: 60.4 us -> none  [the longest x3 39.7 us: attend(): jnp.einsum('bhd,kbhd->hkb', query_block, key_block, preferred_element_typ...]
    reshape x6 -> x0, local copies, waits for them, and re-layouts: 40.4 us -> none  [the longest x3 37.6 us: attend(): picked[:, :model_width].reshape(neighbours, block_rows, HEADS, head_size)]
    select_n x13 -> x1, other arithmetic: 38.3 us -> 1.39 us  [per_device(): target = jnp.where(usable, edge_receiver[:, 0, :], -1)]
    slice x7 -> x0, local copies, waits for them, and re-layouts: 31 us -> none  [the longest x3 21.7 us: attend(): picked[:, :model_width].reshape(neighbours, block_rows, HEADS, head_size)]
    scatter-add x1 -> x0, other arithmetic: 22.9 us -> none  [per_device(): node_acc = jnp.zeros((hidden_units, mesh_rows), jnp.float32).at[:, target...]
  transfers between devices with their start and end apart: 5 -> 0, of which waited for: 5 -> 0; matrix products, arithmetic and copies ran while one was open for 3% -> 0% of each run, Pallas kernels for 0% -> 0%
where the time goes in v2:
time: 115 us
  Pallas kernels  107 us (93%)
  local copies, waits for them, and re-layouts  5.56 us (5%)
  other arithmetic  2.26 us (2%)
    pallas_call x1, Pallas kernels, per_device(): pl.pallas_call(functools.partial(kernel, patches, chans), out_shape=jax.S...  107 us
    unnamed x1, local copies, waits for them, and re-layouts  2.65 us

profile of v2, /device:TPU:0, one launch (start us, length us, event | category | flops | bytes accessed | tf_op | source)
XLA Modules:
  0.0 114.9 jit_solution(5980927002820529682)
XLA Ops:
  0.0 0.9 select_reduce_fusion
  0.9 1.4 %bitcast_select_fusion.target_ref = s32[4,1024]{1,0:T(4,128)} fusion(s32[4,1,1024]{2,1,0:T(1,128)} %param.19, s32[4]{0:T(128)S(1)} %select_reduce_fusion), kind=kLoop, calls=%fused_computation | loop fusion | flops 8192 | bytes 32784 | tf_op jit(solution)/shard_map/jit(_where)/select_n | solution.py:298
  2.3 1.4 %copy.18.bias_ref = f32[128,1]{1,0:T(8,128)} copy(f32[128,1]{0,1:T(1,128)} %bitcast.9) | data formatting | bytes 1024 | tf_op jit(solution)/shard_map/broadcast_in_dim | solution.py:337
  3.6 1.5 %copy.19.gain_ref = f32[512,1]{1,0:T(8,128)} copy(f32[512,1]{0,1:T(1,128)} %bitcast.7) | data formatting | bytes 4096 | tf_op jit(solution)/shard_map/broadcast_in_dim | solution.py:338
  5.2 107.1 %shard_map.154 = bf16[512,1536]{1,0:T(8,128)(2,1)} custom-call(bf16[512,2048]{1,0:T(8,128)(2,1)} %grid_ref.1, bf16[512,1536]{1,0:T(8,128)(2,1)} %mesh_ref.1, s32[4,1024]{1,0:T(4,128)} %bitcast.6, s32[4,1024]{1,0:T(4,128)} %bitcast_select_fusion.target_ref, s32[16,1536]{1,0:T(8,128)} %nbr_ref.1, s32[1,256]{1,0:T(1,128)} %bitcast.8, ...), custom_call_target="tpu_custom_call" | custom-call | tf_op jit(solution)/shard_map/pallas_call | solution.py:300
  112.3 2.7 %copy.23 = bf16[512,1536]{1,0:T(8,128)(2,1)} copy(bf16[512,1536]{1,0:T(8,128)(2,1)} %shard_map.154) | data formatting | bytes 3145728

commit v3 on v2

--- a/solution.py
+++ b/solution.py
@@ -29,6 +29,10 @@
     return jnp.where(ids == index_row - first, 1.0, 0.0).astype(BF16)
 
 
+def column(row):
+    return jnp.broadcast_to(row, (8, row.shape[1])).T[:, :1]
+
+
 def pick_columns(table_ref, index_row):
     picked = None
     for first in range(0, table_ref.shape[1], ONEHOT_ROWS):
@@ -43,13 +47,13 @@
 
 def kernel(
     patches, chans,
-    grid_ref, mesh_ref, sender_ref, target_ref, nbr_ref, offer_ref,
+    grid_ref, mesh_ref, sender_ref, receiver_ref, edge_count_ref, nbr_ref, offer_ref,
     w_send_ref, w_recv_ref, bias_ref, w_edge_out_ref, gain_ref, w_query_ref, w_key_ref,
     w_value_ref, w_attn_out_ref,
     out_ref,
-    sender_table, recv_table, send_buf, recv_buf, received, acc, sums_mine, sums,
+    sender_table, recv_table, send_buf, recv_buf, received, acc, sums,
     w_edge_out, w_attn_out, encoded, query, key, value, offered_acc, offered, halo, count,
-    blended_mine, blended,
+    blended,
     weight_send, weight_recv, edge_send, edge_recv, sum_send, sum_recv, halo_send, halo_recv,
     blend_send, blend_recv,
 ):
@@ -86,6 +90,8 @@
             for off in range(1, chans)
         ]
 
+    bias = column(bias_ref[...])
+    gain = column(gain_ref[...])
     pending = []
 
     def start(copies):
@@ -94,6 +100,69 @@
         pending.extend(copies)
         return copies
 
+    def hop(buffer, block, way, distance, sems):
+        step = 1 - 2 * way
+        source = chan - step * (distance - 1)
+        return pltpu.make_async_remote_copy(
+            src_ref=buffer.at[block, source], dst_ref=buffer.at[block, source],
+            send_sem=sems[0].at[way, block, distance - 1],
+            recv_sem=sems[1].at[way, block, distance - 1],
+            device_id={"chan": chan + step}, device_id_type=pl.DeviceIdType.MESH,
+        )
+
+    def sends(way, distance):
+        if way == 0:
+            return jnp.logical_and(chan >= distance - 1, chan < chans - 1)
+        return jnp.logical_and(chan + distance <= chans, chan > 0)
+
+    def receives(way, distance):
+        return chan >= distance if way == 0 else chan + distance < chans
+
+    def hop_send(buffer, block, distance, sems):
+        for way in range(2):
+
+            @pl.when(sends(way, distance))
+            def _():
+                hop(buffer, block, way, distance, sems).start()
+
+    def hop_wait(buffer, block, distance, sems):
+        for way in range(2):
+
+            @pl.when(receives(way, distance))
+            def _():
+                step = 1 - 2 * way
+                source = chan - step * distance
+                pltpu.make_async_remote_copy(
+                    src_ref=buffer.at[block, source], dst_ref=buffer.at[block, source],
+                    send_sem=sems[0].at[way, block, distance - 1],
+                    recv_sem=sems[1].at[way, block, distance - 1],
+                    device_id={"chan": chan - step}, device_id_type=pl.DeviceIdType.MESH,
+                ).wait_recv()
+
+            if distance < chans - 1:
+
+                @pl.when(sends(way, distance + 1))
+                def _():
+                    hop(buffer, block, way, distance + 1, sems).start()
+
+    def hop_tick(buffer, tick, blocks, sems):
+        for distance in range(1, chans - 1):
+            block = tick - 2 * (distance - 1)
+            if 0 <= block < blocks:
+                hop_wait(buffer, block, distance, sems)
+
+    def hop_finish(buffer, blocks, sems):
+        for block in range(blocks):
+            for distance in range(1, chans):
+                for way in range(2):
+
+                    @pl.when(sends(way, distance))
+                    def _():
+                        hop(buffer, block, way, distance, sems).wait_send()
+
+    sum_sems = (sum_send, sum_recv)
+    blend_sems = (blend_send, blend_recv)
+
     edge_out_copies = start(
         to_chans(w_edge_out_ref, w_edge_out.at[chan], weight_send.at[0], weight_recv.at[0])
     )
@@ -105,7 +174,7 @@
     edge_copies = {}
     for off in offs:
         other = lax.rem(patch + off, patches)
-        send_buf[off] = pick_columns(sender_table, sender_ref[pl.ds(other, 1), :]).astype(BF16)
+        send_buf[off] = pick_columns(sender_table, sender_ref[0, pl.ds(other, 1), :]).astype(BF16)
         edge_copies[off] = pltpu.make_async_remote_copy(
             src_ref=send_buf.at[off], dst_ref=recv_buf.at[off],
             send_sem=edge_send.at[off], recv_sem=edge_recv.at[off],
@@ -115,19 +184,21 @@
     attn_out_copies = start(
         to_chans(w_attn_out_ref, w_attn_out.at[chan], weight_send.at[1], weight_recv.at[1])
     )
-    recv_buf[0] = pick_columns(sender_table, sender_ref[pl.ds(patch, 1), :]).astype(BF16)
+    recv_buf[0] = pick_columns(sender_table, sender_ref[0, pl.ds(patch, 1), :]).astype(BF16)
 
     recv_table[...] = contract0(w_recv_ref[...], mesh_ref[...]).astype(BF16)
     order = [0] + offs
     for off in order:
         band = lax.rem(patch + patches - off, patches)
-        received[off] = pick_columns(recv_table, target_ref[pl.ds(band, 1), :]).astype(BF16)
+        received[off] = pick_columns(recv_table, receiver_ref[band]).astype(BF16)
     for place, off in enumerate(order):
         if off:
             edge_copies[off].wait_recv()
         band = lax.rem(patch + patches - off, patches)
-        index_row = target_ref[pl.ds(band, 1), :]
-        summed = recv_buf[off].astype(F32) + received[off].astype(F32) + bias_ref[...]
+        receivers = receiver_ref[band]
+        slots = lax.broadcasted_iota(jnp.int32, receivers.shape, 1)
+        index_row = jnp.where(slots < edge_count_ref[band, patch], receivers, -1)
+        summed = recv_buf[off].astype(F32) + received[off].astype(F32) + bias
         hidden = (summed / (1.0 + jnp.exp(-summed))).astype(BF16)
         for first in range(0, nodes, ONEHOT_ROWS):
             columns = slice(first, first + ONEHOT_ROWS)
@@ -139,19 +210,9 @@
                 term += acc[:, columns]
             acc[:, columns] = term
 
-    sum_copies = []
     for block in range(node_blocks):
-        node_sum = acc[:, block * NODE_BLOCK : (block + 1) * NODE_BLOCK].astype(BF16)
-        sums_mine[block] = node_sum
-        sum_copies.append(
-            start(
-                to_chans(
-                    sums_mine.at[block], sums.at[block, chan],
-                    sum_send.at[block], sum_recv.at[block],
-                )
-            )
-        )
-        sums[block, chan] = node_sum
+        sums[block, chan] = acc[:, block * NODE_BLOCK : (block + 1) * NODE_BLOCK].astype(BF16)
+        hop_send(sums, block, 1, sum_sems)
 
     def count_block(block):
         index = nbr_ref[:, block * QUERY_BLOCK : (block + 1) * QUERY_BLOCK]
@@ -169,16 +230,18 @@
 
         lax.fori_loop(0, count.shape[1] // COUNT_ROWS, body, 0)
 
-    for block in range(query_blocks - 1):
-        count_block(block)
+    last_lag = max(0, 2 * (chans - 3))
+    for tick in range(max(query_blocks - 1, node_blocks + last_lag)):
+        if tick < query_blocks - 1:
+            count_block(tick)
+        hop_tick(sums, tick, node_blocks, sum_sems)
 
     for copy in edge_out_copies:
         copy.wait_recv()
     head = chan * width // head_size
     columns = pl.ds(pl.multiple_of(head * head_size, head_size), head_size)
     for block in range(node_blocks):
-        for copy in sum_copies[block]:
-            copy.wait_recv()
+        hop_wait(sums, block, chans - 1, sum_sems)
         here = slice(block * NODE_BLOCK, (block + 1) * NODE_BLOCK)
         hidden_units = chans * w_edge_out.shape[1]
         weight = w_edge_out[...].reshape(hidden_units, -1)
@@ -188,24 +251,25 @@
         average = jnp.mean(enc, axis=0, keepdims=True)
         centred = enc - average
         variance = jnp.mean(centred * centred, axis=0, keepdims=True)
-        normed = (centred * lax.rsqrt(variance + 1e-05) * gain_ref[...]).astype(BF16)
+        normed = (centred * lax.rsqrt(variance + 1e-05) * gain).astype(BF16)
         query[:, here] = contract0(w_query_ref[:, columns], normed).astype(BF16)
         block_key = contract0(w_key_ref[:, columns], normed).astype(BF16)
         block_value = contract0(w_value_ref[...], normed).astype(BF16)
         key[here, :] = block_key.T
         value[:, here] = block_value
-        hot = one_hot(block * NODE_BLOCK, NODE_BLOCK, offer_ref[...])
-        key_term = jnp.dot(block_key, hot, preferred_element_type=F32)
-        value_term = jnp.dot(block_value, hot, preferred_element_type=F32)
-        if block:
-            key_term += offered_acc[:head_size]
-            value_term += offered_acc[head_size:]
-        offered_acc[:head_size] = key_term
-        offered_acc[head_size:] = value_term
+        for side in range(2):
+            hot = one_hot(block * NODE_BLOCK, NODE_BLOCK, offer_ref[0, side : side + 1, :])
+            key_term = jnp.dot(block_key, hot, preferred_element_type=F32)
+            value_term = jnp.dot(block_value, hot, preferred_element_type=F32)
+            if block:
+                key_term += offered_acc[side, :head_size]
+                value_term += offered_acc[side, head_size:]
+            offered_acc[side, :head_size] = key_term
+            offered_acc[side, head_size:] = value_term
 
     halo_copies = []
     for side in range(2):
-        offered[side] = offered_acc[:, side * halo_rows : (side + 1) * halo_rows].astype(BF16)
+        offered[side] = offered_acc[side].astype(BF16)
         step = 1 if side == 1 else patches - 1
         halo_copies.append(
             pltpu.make_async_remote_copy(
@@ -224,7 +288,6 @@
         value[:, first : first + halo_rows] = halo[side, head_size:]
         first += halo_rows
 
-    blend_copies = []
     for block in range(query_blocks):
         here = slice(block * QUERY_BLOCK, (block + 1) * QUERY_BLOCK)
         scores = jnp.dot(key[...], query[:, here], preferred_element_type=F32)
@@ -236,22 +299,16 @@
         total = jnp.sum(weight * slots, axis=0, keepdims=True)
         attention = (weight * (1.0 / total)).astype(BF16) * count[block]
         mixed = jnp.dot(value[...], attention, preferred_element_type=F32).astype(BF16)
-        blended_mine[block] = mixed
-        blend_copies.append(
-            start(
-                to_chans(
-                    blended_mine.at[block], blended.at[block, chan],
-                    blend_send.at[block], blend_recv.at[block],
-                )
-            )
-        )
         blended[block, chan] = mixed
+        hop_send(blended, block, 1, blend_sems)
+        hop_tick(blended, block - 1, query_blocks, blend_sems)
+    for tick in range(query_blocks - 1, query_blocks + last_lag):
+        hop_tick(blended, tick, query_blocks, blend_sems)
 
     for copy in attn_out_copies:
         copy.wait_recv()
     for block in range(query_blocks):
-        for copy in blend_copies[block]:
-            copy.wait_recv()
+        hop_wait(blended, block, chans - 1, blend_sems)
         here = slice(block * QUERY_BLOCK, (block + 1) * QUERY_BLOCK)
         rows = chans * w_attn_out.shape[1]
         weight = w_attn_out[...].reshape(rows, -1)
@@ -260,6 +317,8 @@
 
     for copy in pending:
         copy.wait_send()
+    hop_finish(sums, node_blocks, sum_sems)
+    hop_finish(blended, query_blocks, blend_sems)
 
 
 def per_device(
@@ -280,7 +339,6 @@
     w_value,
     w_attn_out,
 ):
-    patch_pos = lax.axis_index("patch")
     patches = lax.axis_size("patch")
     chans = lax.axis_size("chan")
     model_width, nodes = mesh_latent.shape
@@ -293,14 +351,11 @@
     table_rows = nodes + 2 * halo_rows
     node_blocks = nodes // NODE_BLOCK
     query_blocks = nodes // QUERY_BLOCK
-    counts_in = jnp.take(edge_count, patch_pos, axis=1)
-    usable = jnp.arange(capacity, dtype=jnp.int32)[None, :] < counts_in[:, None]
-    target = jnp.where(usable, edge_receiver[:, 0, :], -1)
     sem = lambda *shape: pltpu.SemaphoreType.DMA(shape)
     return pl.pallas_call(
         functools.partial(kernel, patches, chans),
         out_shape=jax.ShapeDtypeStruct((model_width, nodes), BF16),
-        in_specs=[pl.BlockSpec(memory_space=VMEM)] * 15,
+        in_specs=[pl.BlockSpec(memory_space=pltpu.SMEM if i == 4 else VMEM) for i in range(16)],
         out_specs=pl.BlockSpec(memory_space=VMEM),
         scratch_shapes=[
             VMEM((hidden, grid_latent.shape[1]), BF16),
@@ -309,7 +364,6 @@
             VMEM((patches, hidden, capacity), BF16),
             VMEM((patches, hidden, capacity), BF16),
             VMEM((hidden, nodes), F32),
-            VMEM((node_blocks, hidden, NODE_BLOCK), BF16),
             VMEM((node_blocks, chans, hidden, NODE_BLOCK), BF16),
             VMEM((chans,) + w_edge_out.shape, BF16),
             VMEM((chans,) + w_attn_out.shape, BF16),
@@ -317,25 +371,24 @@
             VMEM((head_size, nodes), BF16),
             VMEM((table_rows, head_size), BF16),
             VMEM((width, table_rows), BF16),
-            VMEM((both, 2 * halo_rows), F32),
+            VMEM((2, both, halo_rows), F32),
             VMEM((2, both, halo_rows), BF16),
             VMEM((2, both, halo_rows), BF16),
             VMEM((query_blocks, table_rows, QUERY_BLOCK), BF16),
-            VMEM((query_blocks, width, QUERY_BLOCK), BF16),
             VMEM((query_blocks, chans, width, QUERY_BLOCK), BF16),
             sem(2, chans), sem(2, chans),
             sem(patches), sem(patches),
-            sem(node_blocks, chans), sem(node_blocks, chans),
+            sem(2, node_blocks, chans), sem(2, node_blocks, chans),
             sem(2), sem(2),
-            sem(query_blocks, chans), sem(query_blocks, chans),
+            sem(2, query_blocks, chans), sem(2, query_blocks, chans),
         ],
         compiler_params=pltpu.CompilerParams(
             collective_id=0, has_side_effects=True, vmem_limit_bytes=56 * 2**20
         ),
     )(
-        grid_latent, mesh_latent, edge_sender[0], target, nbr_index,
-        halo_send.reshape(1, -1), w_edge_send, w_edge_recv, b_edge[:, None], w_edge_out,
-        ln_gain[:, None], w_query, w_key, w_value, w_attn_out,
+        grid_latent, mesh_latent, edge_sender, edge_receiver, edge_count, nbr_index,
+        halo_send, w_edge_send, w_edge_recv, b_edge.reshape(1, -1), w_edge_out,
+        ln_gain.reshape(1, -1), w_query, w_key, w_value, w_attn_out,
     )
 
 

time: 115 us -> 93.1 us (0.81)
  Pallas kernels: 107 us -> 90.3 us
  local copies, waits for them, and re-layouts: 5.56 us -> 2.65 us
  other arithmetic: 2.26 us -> 0 us
    pallas_call x1, Pallas kernels: 107 us -> 90.3 us  [per_device(): pl.pallas_call(functools.partial(kernel, patches, chans), out_shape=jax.S...]
    broadcast_in_dim x2 -> x0, local copies, waits for them, and re-layouts: 2.91 us -> none  [the longest x1 1.53 us: per_device(): ln_gain[:, None]]
    select_n x2 -> x0, other arithmetic: 2.26 us -> none  [the longest x1 1.39 us: per_device(): target = jnp.where(usable, edge_receiver[:, 0, :], -1)]
where the time goes in v3:
time: 93.1 us; the launch traced here: 93 us
  Pallas kernels  90.3 us (97%)
  local copies, waits for them, and re-layouts  2.65 us (3%)
    pallas_call x1, Pallas kernels, per_device(): pl.pallas_call(functools.partial(kernel, patches, chans), out_shape=jax.S...  90.3 us
    unnamed x1, local copies, waits for them, and re-layouts  2.65 us

profile of v3, /device:TPU:0, one launch (start us, length us, event | category | flops | bytes accessed | tf_op | source)
XLA Modules:
  0.0 93.0 jit_solution(7010769135895448190)
XLA Ops:
  0.0 90.3 %shard_map.154 = bf16[512,1536]{1,0:T(8,128)(2,1)} custom-call(bf16[512,2048]{1,0:T(8,128)(2,1)} %grid_ref.1, bf16[512,1536]{1,0:T(8,128)(2,1)} %mesh_ref.1, s32[1,4,1024]{2,1,0:T(4,128)} %sender_ref.1, s32[4,1,1024]{2,1,0:T(1,128)} %receiver_ref.1, s32[4,4]{1,0:T(4,128)} %edge_count_ref.1, s32[16,1536]{1,0:T(8,128)} %nbr_ref.1, s32[1,2,128]{2,1,0:T(2,128)} %offer_ref.1, ...), custom_call_target="tpu_custom_call" | custom-call | tf_op jit(solution)/shard_map/pallas_call | solution.py:355
  90.3 2.7 %copy.18 = bf16[512,1536]{1,0:T(8,128)(2,1)} copy(bf16[512,1536]{1,0:T(8,128)(2,1)} %shard_map.154) | data formatting | bytes 3145728
